TPU v7x, 32 devices: a whole 2x2x4 slice. The times are simulated.
32 devices in a mesh: fsdp: 8 (over z, y), tp: 4 (over x, core).
Axes of the slice: x: 2, y: 2, z: 4, core: 2. Of those that a mesh axis runs over, the one named last changes fastest.
Arguments:
- token_ids: int32 [32, 4], replicated, may hold values from 0 to 76031
- lengths: int32 [32], P('fsdp'), may hold values from 64 to 4096, as said below
- embedding: bfloat16 [76032, 8192], P('tp', 'fsdp'), may hold values from -6 to 6
- norm_gain: float32 [8192], replicated, may hold values from 0.1 to 1.9
- w_query: bfloat16 [8192, 4096], P(('fsdp', 'tp')), may hold values from -0.0625 to 0.0625
- w_keyval: bfloat16 [8192, 1024], P(('fsdp', 'tp')), may hold values from -0.15625 to 0.15625
- w_out: bfloat16 [8192, 4096], P(('fsdp', 'tp')), may hold values from -0.09375 to 0.09375
- key_cache: bfloat16 [32, 4096, 512], P('fsdp', None, 'tp'), may hold values from -200 to 200
- value_cache: bfloat16 [32, 4096, 512], P('fsdp', None, 'tp'), may hold values from -15 to 15
Outputs:
- attn_out: bfloat16 [32, 4, 8192], P('fsdp', None, 'tp')
Inputs may be any that keep to these rules, and one draw needn't show every extreme that they name: `lengths`: at least one row has 4096 filled slots and at least one has 64.
All inputs are finite; a program needn't handle non-finite values.
Results may differ from a plain program's by a relative error of at most 0.012.
Values may be sent and summed in bfloat16 or wider, within the bound.
A program may use at most 192 MiB of HBM per device.

v0:
```python
import math

import jax
import jax.numpy as jnp
from jax import lax
from jax.sharding import PartitionSpec as P

HD = 128


EPS_NORM = 1e-06
ROPE_BASE = 1000000.0


def rotate(vectors, positions):
    midpoint = vectors.shape[-1] // 2
    frequency = ROPE_BASE ** (-2.0 * jnp.arange(midpoint, dtype=jnp.float32) / vectors.shape[-1])
    angles = positions.astype(jnp.float32)[..., None, None] * frequency
    cosine = jnp.cos(angles)
    sine_part = jnp.sin(angles)
    leading = vectors[..., :midpoint]
    trailing = vectors[..., midpoint:]
    return jnp.concatenate(
        [leading * cosine - trailing * sine_part, trailing * cosine + leading * sine_part], -1
    )


def contract_last(left, right):
    return lax.dot_general(
        left, right, (((1,), (1,)), ((), ())), preferred_element_type=jnp.float32
    )


def attend(proj_q, proj_kv, lengths, key_cache, value_cache, step_count):
    row_dev = lengths.shape[0]
    context = key_cache.shape[1]
    positions = (lengths[:, None] + jnp.arange(step_count, dtype=jnp.int32)[None, :]).reshape(-1)
    queries = rotate(proj_q.reshape(row_dev * step_count, -1, HD), positions).astype(jnp.bfloat16)
    paired = proj_kv.reshape(row_dev * step_count, -1, 2, HD)
    new_keys = rotate(paired[:, :, 0, :], positions).astype(jnp.bfloat16)
    new_values = paired[:, :, 1, :].astype(jnp.bfloat16)
    kv_heads = key_cache.shape[2] // HD
    group_size = queries.shape[1] // kv_heads
    grouped = queries.reshape(row_dev, step_count, kv_heads, group_size, HD)
    old_keys = key_cache.reshape(row_dev, context, kv_heads, HD)
    old_values = value_cache.reshape(row_dev, context, kv_heads, HD)
    fresh_keys = new_keys.reshape(row_dev, step_count, kv_heads, HD)
    fresh_values = new_values.reshape(row_dev, step_count, kv_heads, HD)
    score_scale = 1.0 / math.sqrt(HD)
    old_scores = (
        jnp.einsum("rsghd,rjgd->rsghj", grouped, old_keys, preferred_element_type=jnp.float32)
        * score_scale
    )
    new_scores = (
        jnp.einsum("rsghd,rtgd->rsght", grouped, fresh_keys, preferred_element_type=jnp.float32)
        * score_scale
    )
    old_seen = (jnp.arange(context, dtype=jnp.int32)[None, :] < lengths[:, None])[
        :, None, None, None, :
    ]
    step_ids = jnp.arange(step_count, dtype=jnp.int32)
    new_seen = (step_ids[None, :] <= step_ids[:, None])[None, :, None, None, :]
    largest = jnp.maximum(
        jnp.max(jnp.where(old_seen, old_scores, -jnp.inf), -1, keepdims=True),
        jnp.max(jnp.where(new_seen, new_scores, -jnp.inf), -1, keepdims=True),
    )
    old_weights = jnp.where(old_seen, jnp.exp(old_scores - largest), 0.0)
    new_weights = jnp.where(new_seen, jnp.exp(new_scores - largest), 0.0)
    totals = jnp.sum(old_weights, -1, keepdims=True) + jnp.sum(new_weights, -1, keepdims=True)
    old_probs = (old_weights / totals).astype(jnp.bfloat16)
    new_probs = (new_weights / totals).astype(jnp.bfloat16)
    blended = jnp.einsum(
        "rsghj,rjgd->rsghd", old_probs, old_values, preferred_element_type=jnp.float32
    )
    blended = blended + jnp.einsum(
        "rsght,rtgd->rsghd", new_probs, fresh_values, preferred_element_type=jnp.float32
    )
    return blended.astype(jnp.bfloat16).reshape(row_dev * step_count, -1)


def on_device(
    token_ids, lengths, embedding, norm_gain, w_query, w_keyval, w_out, key_cache, value_cache
):
    tp_count = lax.axis_size("tp")
    fsdp_count = lax.axis_size("fsdp")
    tp_rank = lax.axis_index("tp")
    fsdp_rank = lax.axis_index("fsdp")
    step_count = token_ids.shape[1]
    row_dev = lengths.shape[0]
    vocab_part = embedding.shape[0]
    token_count = token_ids.size
    depth = w_query.shape[0]
    width = norm_gain.shape[0]
    shifted = token_ids.reshape(-1) - tp_rank * vocab_part
    inside = (shifted >= 0) & (shifted < vocab_part)
    picked = jnp.take(embedding, jnp.clip(shifted, 0, vocab_part - 1), axis=0)
    picked = jnp.where(inside[:, None], picked, jnp.zeros_like(picked))
    parts = lax.all_to_all(
        picked.reshape(token_count, tp_count, depth), "tp", split_axis=1, concat_axis=1, tiled=True
    )
    inputs = jnp.sum(parts.astype(jnp.float32), axis=1)
    gain = lax.dynamic_slice(norm_gain, ((fsdp_rank * tp_count + tp_rank) * depth,), (depth,))
    squares = lax.psum(jnp.sum(inputs * inputs, -1, keepdims=True), ("fsdp", "tp"))
    scale_rows = lax.rsqrt(squares / width + EPS_NORM)
    normed = (inputs * scale_rows * gain).astype(jnp.bfloat16)
    part_q = jnp.dot(normed, w_query, preferred_element_type=jnp.float32)
    part_kv = jnp.dot(normed, w_keyval, preferred_element_type=jnp.float32)
    parts = jnp.concatenate(
        [part_q.reshape(token_count, tp_count, -1), part_kv.reshape(token_count, tp_count, -1)], -1
    )
    mine = lax.psum_scatter(parts, "tp", scatter_dimension=1, tiled=True).reshape(token_count, -1)
    mine = lax.psum_scatter(mine, "fsdp", scatter_dimension=0, tiled=True)
    q_cols = w_query.shape[1] // tp_count
    attended = attend(
        mine[:, :q_cols], mine[:, q_cols:], lengths, key_cache, value_cache, step_count
    )
    everything = lax.all_gather(attended, "fsdp", axis=0, tiled=True)
    everything = lax.all_gather(everything, "tp", axis=1, tiled=True)
    features = contract_last(everything, w_out).astype(jnp.bfloat16)
    rows = lax.all_to_all(features, "fsdp", split_axis=0, concat_axis=1, tiled=True)
    near = fsdp_count // tp_count
    rows = rows.reshape(row_dev * step_count, tp_count, near, 1, depth)
    rows = lax.all_to_all(rows, "tp", split_axis=1, concat_axis=3, tiled=True)
    return rows.reshape(row_dev, step_count, -1)


def solution(mesh):
    return jax.shard_map(
        on_device,
        mesh=mesh,
        in_specs=(
            P(),
            P("fsdp"),
            P("tp", "fsdp"),
            P(),
            P(("fsdp", "tp"), None),
            P(("fsdp", "tp"), None),
            P(("fsdp", "tp"), None),
            P("fsdp", None, "tp"),
            P("fsdp", None, "tp"),
        ),
        out_specs=P("fsdp", None, "tp"),
        check_vma=False,
    )
```

profile of v0, /device:TPU:3, one launch (start us, length us, event | category | flops | bytes accessed | tf_op | source)
XLA Modules:
  0.0 252.7 jit_solution(6423149339613803762)
XLA Ops:
  6.5 0.0 copy-start
  6.5 0.8 subtract_clamp_fusion
  7.4 0.1 copy.41
  7.5 0.1 min.18
  7.6 0.1 min.16
  7.7 0.7 compare_and_fusion.1
  8.4 0.1 copy.40
  8.5 0.1 and.20
  8.6 5.2 %gather_fusion = bf16[128,1024]{1,0:T(8,128)(2,1)S(1)} fusion(bf16[19008,1024]{1,0:T(8,128)(2,1)} %param.11, s32[1024]{0:T(1024)S(1)} %pad_clamp_fusion), kind=kCustom, calls=%fused_computation | custom fusion | bytes 524800 | tf_op jit(solution)/shard_map/jit(_take)/gather | solution.py:96
  13.8 0.8 fusion.20
  14.6 3.4 %all-to-all-start = ((bf16[128,4,256]{2,0,1:T(8,128)(2,1)}), bf16[128,4,256]{2,0,1:T(8,128)(2,1)S(1)}, u32[]{:S(2)}, u32[]{:S(2)}) async-start(bf16[128,4,256]{2,0,1:T(8,128)(2,1)} %fusion.20), calls=%async_computation | async-start | bytes 524288 | tf_op jit(solution)/shard_map/all_to_all | solution.py:98
  18.0 0.0 reduce-scatter.3.cloned.1.call-start
  18.1 0.8 dynamic_slice.3
  18.9 3.0 %all-to-all-done = bf16[128,4,256]{2,0,1:T(8,128)(2,1)S(1)} async-done(((bf16[128,4,256]{2,0,1:T(8,128)(2,1)}), bf16[128,4,256]{2,0,1:T(8,128)(2,1)S(1)}, u32[]{:S(2)}, u32[]{:S(2)}) %all-to-all-start) | async-done | bytes 262176 | tf_op jit(solution)/shard_map/all_to_all | solution.py:98
  21.9 0.1 multiply_reduce_fusion
  22.0 41.8 %psum.7 = f32[128,1]{0,1:T(1,128)S(1)} all-reduce(f32[128,1]{0,1:T(1,128)S(1)} %bitcast.130), channel_id=1, replica_groups=mesh['fsdp'=8,'tp'=4] {'fsdp','tp'}, use_global_device_ids=true, to_apply=%region_2.3 | all-reduce | flops 128 | bytes 1024 | tf_op jit(solution)/shard_map/psum | solution.py:103
  63.8 0.0 copy-done
  63.8 0.5 fusion.43
  64.3 0.0 copy-start.1
  64.3 0.1 copy.68
  64.4 0.9 copy-done.1
  65.3 0.3 fusion.42
  65.7 1.7 pad_maximum_fusion
  67.4 0.0 copy-start.2
  67.4 0.0 reduce-scatter.3.cloned.1.call-update
  67.4 0.0 reduce-scatter.5.cloned.1.call-start
  67.4 0.6 copy-done.2
  68.0 0.1 add_convert_fusion.1
  68.1 0.1 convert_element_type.55
  68.2 33.8 %reduce-scatter.3.cloned.1.call-done = f32[128,1,1280]{2,0,1:T(8,128)} async-done(((f32[128,4,1280]{2,0,1:T(8,128)}), f32[128,1,1280]{2,0,1:T(8,128)}) %reduce-scatter.3.cloned.1.call-update) | async-done | bytes 655376 | tf_op jit(solution)/shard_map/reduce_scatter | solution.py:111
  101.9 0.0 reduce-scatter.5.cloned.1.call-update
  102.0 0.0 all-gather.2.cloned.1.call-start
  102.0 0.1 multiply_cosine_fusion.1
  102.2 0.1 iota_compare_fusion
  102.3 64.7 %reduce-scatter.5.cloned.1.call-done = f32[16,1280]{1,0:T(8,128)} async-done(((f32[128,1280]{1,0:T(8,128)}), f32[16,1280]{1,0:T(8,128)}) %reduce-scatter.5.cloned.1.call-update) | async-done | bytes 81936 | tf_op jit(solution)/shard_map/reduce_scatter | solution.py:112
  167.0 0.7 slice.38
  167.8 0.8 slice_bitcast_fusion
  168.6 0.1 fusion.32
  168.8 0.1 subtract_convert_fusion
  168.9 0.0 copy-start.3
  168.9 4.0 %select_reduce_fusion = (f32[4,4,8]{2,1,0:T(4,128)S(1)}, f32[4,1,4096,4,8]{2,4,3,0,1:T(8,128)S(1)}) fusion(pred[4,4096]{1,0:T(4,128)(4,1)S(1)} %iota_compare_fusion, bf16[4,4096,128]{2,1,0:T(8,128)(2,1)} %param.16, bf16[4,4,8,64]{3,2,1,0:T(8,128)(2,1)S(1)} %bitcast.122, bf16[4,4,8,64]{3,2,1,0:T(8,128)(2,1)S(1)} %bitcast.120), kind=kOutput, calls=%fused_computation.12 | convolution fusion | flops 135856000 | bytes 6341120 | tf_op jit(solution)/shard_map/rsghd,rjgd->rsghj/dot_general | solution.py:51
  172.9 0.3 select_reduce_fusion.1
  173.2 0.1 fusion.21
  173.3 0.6 bitcast_reduce_fusion
  173.9 0.3 fusion.22
  174.2 0.0 copy-done.3
  174.2 0.9 fusion.11
  175.1 26.4 %all_gather.6 = bf16[128,1024]{1,0:T(8,128)(2,1)} all-gather(bf16[16,1024]{1,0:T(8,128)(2,1)S(1)} %bitcast.124), channel_id=1, replica_groups=mesh['fsdp'=8,'tp'=4] {'fsdp'}, dimensions={0}, use_global_device_ids=true | all-gather | bytes 294912 | tf_op jit(solution)/shard_map/all_gather | solution.py:117
  201.5 0.0 all-gather.2.cloned.1.call-update
  201.5 23.2 %all-gather.2.cloned.1.call-done = bf16[128,4096]{1,0:T(8,128)(2,1)} async-done(((bf16[128,1024]{1,0:T(8,128)(2,1)}), bf16[128,4096]{1,0:T(8,128)(2,1)}) %all-gather.2.cloned.1.call-update) | async-done | bytes 1048592 | tf_op jit(solution)/shard_map/all_gather | solution.py:118
  224.7 2.8 %convolution_convert_fusion = bf16[128,256]{1,0:T(8,128)(2,1)S(1)} fusion(bf16[128,4096]{1,0:T(8,128)(2,1)} %all-gather.2.cloned.1.call-done, bf16[256,4096]{1,0:T(8,128)(2,1)} %param.15), kind=kOutput, calls=%fused_computation.13 | convolution fusion | flops 268468224 | bytes 3211264 | tf_op jit(solution)/shard_map/dot_general | solution.py:29
  227.5 11.1 %all_to_all.36 = bf16[8,16,256]{2,1,0:T(8,128)(2,1)S(1)} all-to-all(bf16[8,16,256]{2,1,0:T(8,128)(2,1)S(1)} %bitcast.117), channel_id=1, replica_groups=mesh['fsdp'=8,'tp'=4] {'fsdp'}, dimensions={0} | all-to-all | bytes 131072 | tf_op jit(solution)/shard_map/all_to_all | solution.py:120
  238.5 0.1 copy.48
  238.6 6.9 %all_to_all.37 = bf16[16,4,2,1,256]{4,2,0,3,1:T(2,128)(2,1)S(1)} all-to-all(bf16[16,4,2,1,256]{4,2,0,3,1:T(2,128)(2,1)S(1)} %copy.48), channel_id=1, replica_groups=mesh['fsdp'=8,'tp'=4] {'tp'}, dimensions={1} | all-to-all | bytes 131072 | tf_op jit(solution)/shard_map/all_to_all | solution.py:123
  245.5 0.1 copy.49
  245.5 0.7 reshape.355
  (17 shorter events, 0.2 us)
Async XLA Ops:
  6.5 57.3 %copy-start = (bf16[256,4096]{1,0:T(8,128)(2,1)S(1)}, bf16[256,4096]{1,0:T(8,128)(2,1)}, u32[]{:S(2)}) copy-start(bf16[256,4096]{1,0:T(8,128)(2,1)} %param.13) | copy-start | bytes 6291460
  14.6 7.2 %all-to-all-start = ((bf16[128,4,256]{2,0,1:T(8,128)(2,1)}), bf16[128,4,256]{2,0,1:T(8,128)(2,1)S(1)}, u32[]{:S(2)}, u32[]{:S(2)}) async-start(bf16[128,4,256]{2,0,1:T(8,128)(2,1)} %fusion.20), calls=%async_computation | async-start | bytes 524288 | tf_op jit(solution)/shard_map/all_to_all | solution.py:98
  18.0 83.9 %reduce-scatter.3.cloned.1.call-start = ((), (), s32[]{:S(2)}) async-start(), calls=%async_computation.5 | async-start | bytes 3276800 | tf_op jit(solution)/shard_map/reduce_scatter | solution.py:111
  64.3 1.0 copy-start.1
  67.4 0.7 copy-start.2
  67.4 99.6 %reduce-scatter.5.cloned.1.call-start = ((), (), s32[]{:S(2)}) async-start(), calls=%async_computation.6 | async-start | bytes 737280 | tf_op jit(solution)/shard_map/reduce_scatter | solution.py:112
  102.0 122.7 %all-gather.2.cloned.1.call-start = ((), (), s32[]{:S(2)}) async-start(), calls=%async_computation.7 | async-start | bytes 1310720 | tf_op jit(solution)/shard_map/all_gather | solution.py:118
  168.9 5.3 %copy-start.3 = (bf16[4,4096,128]{2,1,0:T(8,128)(2,1)S(1)}, bf16[4,4096,128]{2,1,0:T(8,128)(2,1)}, u32[]{:S(2)}) copy-start(bf16[4,4096,128]{2,1,0:T(8,128)(2,1)} %param.17) | copy-start | bytes 12582916
Sparse Core Ops, SparseCore 0:
  67.5 34.3 reduce-scatter.2
  105.6 61.3 reduce-scatter.4
  201.6 23.0 all-gather.1
where the time goes:
time: 256 us; the launch traced here: 253 us
  waiting for transfers between devices  125 us (49%)
  blocking collectives  86.1 us (34%)
  between operations  13.3 us (5%)
  local copies, waits for them, and re-layouts  10.6 us (4%)
  matrix products  8.97 us (4%)
  other arithmetic  5.4 us (2%)
  starting transfers between devices  3.52 us (1%)
    reduce_scatter x1, waiting for transfers between devices, on_device(): mine = lax.psum_scatter(mine, 'fsdp', scatter_dimension=0, tiled=True)  64.7 us
    psum x1, blocking collectives, on_device(): lax.psum(jnp.sum(inputs * inputs, -1, keepdims=True), ('fsdp', 'tp'))  41.8 us
    reduce_scatter x1, waiting for transfers between devices, on_device(): lax.psum_scatter(parts, 'tp', scatter_dimension=1, tiled=True)  33.8 us
    all_gather x1, blocking collectives, on_device(): everything = lax.all_gather(attended, 'fsdp', axis=0, tiled=True)  26.4 us
    all_gather x1, waiting for transfers between devices, on_device(): everything = lax.all_gather(everything, 'tp', axis=1, tiled=True)  23.2 us
    all_to_all x1, blocking collectives, on_device(): lax.all_to_all(features, 'fsdp', split_axis=0, concat_axis=1, tiled=True)  11.1 us
    all_to_all x1, blocking collectives, on_device(): rows = lax.all_to_all(rows, 'tp', split_axis=1, concat_axis=3, tiled=True)  6.92 us
    gather x1, local copies, waits for them, and re-layouts, on_device(): picked = jnp.take(embedding, jnp.clip(shifted, 0, vocab_part - 1), axis=0)  5.21 us
  transfers between devices with their start and end apart: 4, of which 4 were waited for; matrix products, arithmetic and copies ran while one was open for 0% of the time, Pallas kernels for 0%

commit v1 on v0

--- a/solution.py
+++ b/solution.py
@@ -1,8 +1,11 @@
+import functools
 import math
 
 import jax
 import jax.numpy as jnp
 from jax import lax
+from jax.experimental import pallas as pl
+from jax.experimental.pallas import tpu as pltpu
 from jax.sharding import PartitionSpec as P
 
 HD = 128
@@ -78,6 +81,369 @@
     return blended.astype(jnp.bfloat16).reshape(row_dev * step_count, -1)
 
 
+MESH = pl.DeviceIdType.MESH
+VMEM_LIMIT = 48 * 1024 * 1024
+
+
+def remote(src, dst, send_sem, recv_sem, device):
+    return pltpu.make_async_remote_copy(
+        src_ref=src,
+        dst_ref=dst,
+        send_sem=send_sem,
+        recv_sem=recv_sem,
+        device_id=device,
+        device_id_type=MESH,
+    )
+
+
+def greet_all(me, count, tp_count):
+    barrier = pltpu.get_barrier_semaphore()
+
+    def greet(step, carry):
+        other = lax.rem(me + step, count)
+        pl.semaphore_signal(
+            barrier, inc=1, device_id=(other // tp_count, lax.rem(other, tp_count)), device_id_type=MESH
+        )
+        return carry
+
+    lax.fori_loop(1, count, greet, 0)
+    pl.semaphore_wait(barrier, count - 1)
+
+
+def project_kernel(
+    fsdp_count, tp_count, picked, squares, gain, w_query, w_keyval, mine,
+    wq_buf, wkv_buf, x_buf, sq_buf, away, kept, from_core, plane_out, from_plane, line_out, from_line,
+    w_sem, x_send, x_recv, sq_send, sq_recv, core_send, core_recv, plane_send, plane_recv,
+    line_send, line_recv,
+):
+    f = lax.axis_index("fsdp")
+    t = lax.axis_index("tp")
+    count = fsdp_count * tp_count
+    me = f * tp_count + t
+    fz, fy = f // 2, lax.rem(f, 2)
+    xi, core = t // 2, lax.rem(t, 2)
+    lines = fsdp_count // 2
+    query_copy = pltpu.make_async_copy(w_query, wq_buf, w_sem.at[0])
+    keyval_copy = pltpu.make_async_copy(w_keyval, wkv_buf, w_sem.at[1])
+    query_copy.start()
+    keyval_copy.start()
+    greet_all(me, count, tp_count)
+
+    def x_copy(step):
+        other = lax.rem(t + step, tp_count)
+        return remote(
+            picked.at[other], x_buf.at[step - 1], x_send.at[step - 1], x_recv.at[step - 1], (f, other)
+        )
+
+    def sq_copy(step):
+        other = lax.rem(me + step, count)
+        return remote(
+            squares, sq_buf.at[step - 1], sq_send.at[step - 1], sq_recv.at[step - 1],
+            (other // tp_count, lax.rem(other, tp_count)),
+        )
+
+    for step in range(1, tp_count):
+        x_copy(step).start()
+
+    def send_sq(step, carry):
+        sq_copy(step).start()
+        return carry
+
+    lax.fori_loop(1, count, send_sq, 0)
+    inputs = picked[t].astype(jnp.float32)
+    for step in range(1, tp_count):
+        x_copy(step).wait_recv()
+        inputs = inputs + x_buf[step - 1].astype(jnp.float32)
+
+    def take_sq(step, total):
+        sq_copy(step).wait_recv()
+        return total + sq_buf[step - 1]
+
+    total = lax.fori_loop(1, count, take_sq, squares[...])
+    tokens, depth = inputs.shape
+    column = jnp.transpose(jnp.broadcast_to(total[:1], (128, tokens)))[:, :1]
+    scale_rows = lax.rsqrt(column / (depth * count) + EPS_NORM)
+    normed = (inputs * scale_rows * gain[...]).astype(jnp.bfloat16)
+    query_copy.wait()
+    keyval_copy.wait()
+    q_cols = wq_buf.shape[1] // tp_count
+    kv_cols = wkv_buf.shape[1] // tp_count
+
+    def project(head, store):
+        for lo in range(0, q_cols, 512):
+            columns = pl.ds(pl.multiple_of(head * q_cols + lo, 128), min(512, q_cols - lo))
+            store(lo, jnp.dot(normed, wq_buf[:, columns], preferred_element_type=jnp.float32))
+        columns = pl.ds(pl.multiple_of(head * kv_cols, 128), kv_cols)
+        store(q_cols, jnp.dot(normed, wkv_buf[:, columns], preferred_element_type=jnp.float32))
+
+    def core_copy(side):
+        return remote(
+            away.at[side], from_core.at[side], core_send.at[side], core_recv.at[side], (f, xi * 2 + 1 - core)
+        )
+
+    order = (lax.rem(xi + 1, 2), xi)
+    for place in range(2):
+        def store(lo, value, place=place):
+            away[place, :, lo : lo + value.shape[1]] = value.astype(jnp.bfloat16)
+
+        project(order[place] * 2 + 1 - core, store)
+
+    for place in range(2):
+        core_copy(place).start()
+    for place in range(2):
+        def store(lo, value, place=place):
+            kept[place, :, lo : lo + value.shape[1]] = value
+
+        project(order[place] * 2 + core, store)
+    half = tokens // 2
+
+    def plane_copy(dx, dy):
+        slot = dx * 2 + dy - 1
+        return remote(
+            plane_out.at[slot], from_plane.at[slot], plane_send.at[slot], plane_recv.at[slot],
+            (fz * 2 + lax.rem(fy + dy, 2), lax.rem(xi + dx, 2) * 2 + core),
+        )
+
+    core_copy(0).wait_recv()
+    for dy in (1, 0):
+        rows = pl.ds(pl.multiple_of(lax.rem(fy + dy, 2) * half, 16), half)
+        plane_out[2 + dy - 1] = (
+            kept[0, rows, :] + from_core[0, rows, :].astype(jnp.float32)
+        ).astype(jnp.bfloat16)
+        plane_copy(1, dy).start()
+    core_copy(1).wait_recv()
+    rows = pl.ds(pl.multiple_of(lax.rem(fy + 1, 2) * half, 16), half)
+    plane_out[0] = (kept[1, rows, :] + from_core[1, rows, :].astype(jnp.float32)).astype(jnp.bfloat16)
+    plane_copy(0, 1).start()
+    rows = pl.ds(pl.multiple_of(fy * half, 16), half)
+    own = kept[1, rows, :] + from_core[1, rows, :].astype(jnp.float32)
+    plane_copy(0, 1).wait_recv()
+    own = own + from_plane[0].astype(jnp.float32)
+    plane_copy(1, 0).wait_recv()
+    own = own + from_plane[1].astype(jnp.float32)
+    plane_copy(1, 1).wait_recv()
+    own = own + from_plane[2].astype(jnp.float32)
+    block = half // lines
+    kept[0, :half, :] = own
+    line_out[...] = own.astype(jnp.bfloat16).reshape(line_out.shape)
+
+    def line_copy(step):
+        other = lax.rem(fz + step, lines)
+        return remote(
+            line_out.at[other], from_line.at[step - 1], line_send.at[step - 1], line_recv.at[step - 1],
+            (other * 2 + fy, t),
+        )
+
+    for step in range(1, lines):
+        line_copy(step).start()
+    result = kept[0, pl.ds(pl.multiple_of(fz * block, 16), block), :]
+    for step in range(1, lines):
+        line_copy(step).wait_recv()
+        result = result + from_line[step - 1].astype(jnp.float32)
+    mine[...] = result
+    for step in range(1, tp_count):
+        x_copy(step).wait_send()
+
+    def done_sq(step, carry):
+        sq_copy(step).wait_send()
+        return carry
+
+    lax.fori_loop(1, count, done_sq, 0)
+    for place in range(2):
+        core_copy(place).wait_send()
+    plane_copy(0, 1).wait_send()
+    plane_copy(1, 0).wait_send()
+    plane_copy(1, 1).wait_send()
+    for step in range(1, lines):
+        line_copy(step).wait_send()
+
+
+def project(fsdp_count, tp_count, picked, squares, gain, w_query, w_keyval):
+    _, tokens, depth = picked.shape
+    count = fsdp_count * tp_count
+    lines = fsdp_count // 2
+    cols = (w_query.shape[1] + w_keyval.shape[1]) // tp_count
+    half = tokens // 2
+    dma = pltpu.SemaphoreType.DMA
+    bf16, f32 = jnp.bfloat16, jnp.float32
+    vmem = pl.BlockSpec(memory_space=pltpu.VMEM)
+    hbm = pl.BlockSpec(memory_space=pl.ANY)
+    return pl.pallas_call(
+        functools.partial(project_kernel, fsdp_count, tp_count),
+        out_shape=jax.ShapeDtypeStruct((tokens // fsdp_count, cols), f32),
+        in_specs=[vmem, vmem, vmem, hbm, hbm],
+        out_specs=vmem,
+        scratch_shapes=[
+            pltpu.VMEM(w_query.shape, bf16),
+            pltpu.VMEM(w_keyval.shape, bf16),
+            pltpu.VMEM((tp_count - 1, tokens, depth), bf16),
+            pltpu.VMEM((count - 1,) + squares.shape, f32),
+            pltpu.VMEM((2, tokens, cols), bf16),
+            pltpu.VMEM((2, tokens, cols), f32),
+            pltpu.VMEM((2, tokens, cols), bf16),
+            pltpu.VMEM((3, half, cols), bf16),
+            pltpu.VMEM((3, half, cols), bf16),
+            pltpu.VMEM((lines, half // lines, cols), bf16),
+            pltpu.VMEM((lines - 1, half // lines, cols), bf16),
+            dma((2,)),
+            dma((tp_count - 1,)), dma((tp_count - 1,)),
+            dma((count - 1,)), dma((count - 1,)),
+            dma((2,)), dma((2,)),
+            dma((3,)), dma((3,)),
+            dma((lines - 1,)), dma((lines - 1,)),
+        ],
+        compiler_params=pltpu.CompilerParams(
+            collective_id=0, has_side_effects=True, vmem_limit_bytes=VMEM_LIMIT
+        ),
+        name="project",
+    )(picked, squares, gain, w_query, w_keyval)
+
+
+def output_kernel(
+    fsdp_count, tp_count, attended, w_out, got,
+    w_buf, parts, sums, blocks, gathered,
+    w_sem, line_send, line_recv, plane_send, plane_recv, core_send, core_recv, out_send, out_recv,
+):
+    f = lax.axis_index("fsdp")
+    t = lax.axis_index("tp")
+    count = fsdp_count * tp_count
+    fz, fy = f // 2, lax.rem(f, 2)
+    xi, core = t // 2, lax.rem(t, 2)
+    lines = fsdp_count // 2
+    near = fsdp_count // tp_count
+    weight_copy = pltpu.make_async_copy(w_out, w_buf, w_sem)
+    weight_copy.start()
+    parts[core, xi, fy, fz] = attended[...]
+    greet_all(f * tp_count + t, count, tp_count)
+
+    def line_copy(step, source):
+        other = lax.rem(fz + step, lines)
+        spot = parts.at[core, xi, fy, source]
+        return remote(spot, spot, line_send.at[step - 1], line_recv.at[step - 1], (other * 2 + fy, t))
+
+    def plane_copy(dx, dy, back):
+        slot = dx * 2 + dy - 1
+        other_x, other_y = lax.rem(xi + dx, 2), lax.rem(fy + dy, 2)
+        spot = parts.at[core, other_x, other_y] if back else parts.at[core, xi, fy]
+        return remote(
+            spot, spot, plane_send.at[slot], plane_recv.at[slot], (fz * 2 + other_y, other_x * 2 + core)
+        )
+
+    def core_copy(dx, dy, back):
+        slot = dx * 2 + dy
+        side = 1 - core if back else core
+        spot = parts.at[side, lax.rem(xi + dx, 2), lax.rem(fy + dy, 2)]
+        return remote(spot, spot, core_send.at[slot], core_recv.at[slot], (f, xi * 2 + 1 - core))
+
+    for step in range(1, lines):
+        line_copy(step, fz).start()
+    for step in range(1, lines):
+        line_copy(step, lax.rem(fz - step + lines, lines)).wait_recv()
+    peers = ((1, 1), (1, 0), (0, 1))
+    for dx, dy in peers:
+        plane_copy(dx, dy, False).start()
+    core_copy(0, 0, False).start()
+    for dx, dy in reversed(peers):
+        plane_copy(dx, dy, True).wait_recv()
+        core_copy(dx, dy, False).start()
+    weight_copy.wait()
+    tokens = sums.shape[0]
+    cols = w_buf.shape[1] // tp_count
+
+    def add(side, far, first):
+        columns = pl.ds(pl.multiple_of((far * 2 + side) * cols, 128), cols)
+        value = contract_last(parts[side, far].reshape(tokens, cols), w_buf[:, columns])
+        if first:
+            sums[...] = value
+        else:
+            sums[...] += value
+
+    add(core, xi, True)
+    add(core, lax.rem(xi + 1, 2), False)
+    for dx, dy in ((0, 0),) + tuple(reversed(peers)):
+        core_copy(dx, dy, True).wait_recv()
+    add(1 - core, xi, False)
+    add(1 - core, lax.rem(xi + 1, 2), False)
+    blocks[...] = sums[...].astype(jnp.bfloat16).reshape(blocks.shape)
+    target = f // near
+    place = lax.rem(f, near) * tp_count + t
+
+    def out_copy(step):
+        other = lax.rem(f + step, fsdp_count)
+        return remote(
+            blocks.at[lax.rem(other, 2) * lines + other // 2], gathered.at[place],
+            out_send.at[step], out_recv.at[place], (other, target),
+        )
+
+    for step in range(1, fsdp_count):
+        out_copy(step).start()
+
+    @pl.when(target != t)
+    def _():
+        out_copy(0).start()
+
+    @pl.when(target == t)
+    def _():
+        gathered[place] = blocks[fy * lines + fz]
+
+    def source(slot):
+        return t * near + slot // tp_count, slot % tp_count
+
+    for slot in range(near * tp_count):
+        sender_f, sender_t = source(slot)
+
+        @pl.when(jnp.logical_or(sender_f != f, sender_t != t))
+        def _(slot=slot, sender_f=sender_f, sender_t=sender_t):
+            remote(
+                blocks.at[0], gathered.at[slot], out_send.at[0], out_recv.at[slot], (sender_f, sender_t)
+            ).wait_recv()
+
+    got[...] = gathered[...]
+    for step in range(1, lines):
+        line_copy(step, fz).wait_send()
+    for dx, dy in peers:
+        plane_copy(dx, dy, False).wait_send()
+    for dx, dy in ((0, 0),) + peers:
+        core_copy(dx, dy, False).wait_send()
+    for step in range(1, fsdp_count):
+        out_copy(step).wait_send()
+
+    @pl.when(target != t)
+    def _():
+        out_copy(0).wait_send()
+
+
+def output(fsdp_count, tp_count, attended, w_out):
+    row_tokens, cols = attended.shape
+    depth = w_out.shape[0]
+    lines = fsdp_count // 2
+    slots = (fsdp_count // tp_count) * tp_count
+    dma = pltpu.SemaphoreType.DMA
+    vmem = pl.BlockSpec(memory_space=pltpu.VMEM)
+    return pl.pallas_call(
+        functools.partial(output_kernel, fsdp_count, tp_count),
+        out_shape=jax.ShapeDtypeStruct((slots, row_tokens, depth), jnp.bfloat16),
+        in_specs=[vmem, pl.BlockSpec(memory_space=pl.ANY)],
+        out_specs=vmem,
+        scratch_shapes=[
+            pltpu.VMEM(w_out.shape, jnp.bfloat16),
+            pltpu.VMEM((2, 2, 2, lines, row_tokens, cols), jnp.bfloat16),
+            pltpu.VMEM((fsdp_count * row_tokens, depth), jnp.float32),
+            pltpu.VMEM((fsdp_count, row_tokens, depth), jnp.bfloat16),
+            pltpu.VMEM((slots, row_tokens, depth), jnp.bfloat16),
+            dma,
+            dma((lines - 1,)), dma((lines - 1,)),
+            dma((3,)), dma((3,)),
+            dma((4,)), dma((4,)),
+            dma((fsdp_count,)), dma((slots,)),
+        ],
+        compiler_params=pltpu.CompilerParams(
+            collective_id=1, has_side_effects=True, vmem_limit_bytes=VMEM_LIMIT
+        ),
+        name="output",
+    )(attended, w_out)
+
+
 def on_device(
     token_ids, lengths, embedding, norm_gain, w_query, w_keyval, w_out, key_cache, value_cache
 ):
@@ -90,38 +456,22 @@
     vocab_part = embedding.shape[0]
     token_count = token_ids.size
     depth = w_query.shape[0]
-    width = norm_gain.shape[0]
-    shifted = token_ids.reshape(-1) - tp_rank * vocab_part
+    ordered = token_ids.reshape(fsdp_count // 2, 2, -1).transpose(1, 0, 2).reshape(-1)
+    shifted = ordered - tp_rank * vocab_part
     inside = (shifted >= 0) & (shifted < vocab_part)
     picked = jnp.take(embedding, jnp.clip(shifted, 0, vocab_part - 1), axis=0)
     picked = jnp.where(inside[:, None], picked, jnp.zeros_like(picked))
-    parts = lax.all_to_all(
-        picked.reshape(token_count, tp_count, depth), "tp", split_axis=1, concat_axis=1, tiled=True
-    )
-    inputs = jnp.sum(parts.astype(jnp.float32), axis=1)
+    wide = picked.astype(jnp.float32)
+    squares = jnp.broadcast_to(jnp.sum(wide * wide, -1)[None, :], (8, token_count))
+    picked = picked.reshape(token_count, tp_count, depth).transpose(1, 0, 2)
     gain = lax.dynamic_slice(norm_gain, ((fsdp_rank * tp_count + tp_rank) * depth,), (depth,))
-    squares = lax.psum(jnp.sum(inputs * inputs, -1, keepdims=True), ("fsdp", "tp"))
-    scale_rows = lax.rsqrt(squares / width + EPS_NORM)
-    normed = (inputs * scale_rows * gain).astype(jnp.bfloat16)
-    part_q = jnp.dot(normed, w_query, preferred_element_type=jnp.float32)
-    part_kv = jnp.dot(normed, w_keyval, preferred_element_type=jnp.float32)
-    parts = jnp.concatenate(
-        [part_q.reshape(token_count, tp_count, -1), part_kv.reshape(token_count, tp_count, -1)], -1
-    )
-    mine = lax.psum_scatter(parts, "tp", scatter_dimension=1, tiled=True).reshape(token_count, -1)
-    mine = lax.psum_scatter(mine, "fsdp", scatter_dimension=0, tiled=True)
+    mine = project(fsdp_count, tp_count, picked, squares, gain[None, :], w_query, w_keyval)
     q_cols = w_query.shape[1] // tp_count
     attended = attend(
         mine[:, :q_cols], mine[:, q_cols:], lengths, key_cache, value_cache, step_count
     )
-    everything = lax.all_gather(attended, "fsdp", axis=0, tiled=True)
-    everything = lax.all_gather(everything, "tp", axis=1, tiled=True)
-    features = contract_last(everything, w_out).astype(jnp.bfloat16)
-    rows = lax.all_to_all(features, "fsdp", split_axis=0, concat_axis=1, tiled=True)
-    near = fsdp_count // tp_count
-    rows = rows.reshape(row_dev * step_count, tp_count, near, 1, depth)
-    rows = lax.all_to_all(rows, "tp", split_axis=1, concat_axis=3, tiled=True)
-    return rows.reshape(row_dev, step_count, -1)
+    rows = output(fsdp_count, tp_count, attended, w_out)
+    return rows.transpose(1, 0, 2).reshape(row_dev, step_count, -1)
 
 
 def solution(mesh):

time: 256 us -> 69.8 us (0.27); the launches traced: 253 us -> 69.3 us
  waiting for transfers between devices: 125 us -> 0 us
  blocking collectives: 86.1 us -> 0 us
  Pallas kernels: 0 us -> 50.5 us
  between operations: 13.3 us -> 0.23 us
  starting transfers between devices: 3.52 us -> 0 us
  matrix products: 8.97 us -> 5.49 us
    reduce_scatter x2 -> x0, waiting for transfers between devices: 98.5 us -> none  [the longest x1 64.7 us: on_device(): mine = lax.psum_scatter(mine, 'fsdp', scatter_dimension=0, tiled=True)]
    pallas_call x0 -> x2, Pallas kernels: none -> 50.5 us  [the longest x1 28 us: project(): pl.pallas_call(functools.partial(project_kernel, fsdp_count, tp_count), o...]
    psum x1 -> x0, blocking collectives: 41.8 us -> none  [on_device(): lax.psum(jnp.sum(inputs * inputs, -1, keepdims=True), ('fsdp', 'tp'))]
    all_gather x1 -> x0, blocking collectives: 26.4 us -> none  [on_device(): everything = lax.all_gather(attended, 'fsdp', axis=0, tiled=True)]
    all_gather x1 -> x0, waiting for transfers between devices: 23.2 us -> none  [on_device(): everything = lax.all_gather(everything, 'tp', axis=1, tiled=True)]
    all_to_all x2 -> x0, blocking collectives: 18 us -> none  [the longest x1 11.1 us: on_device(): lax.all_to_all(features, 'fsdp', split_axis=0, concat_axis=1, tiled=True)]
    dot_general x3 -> x0, matrix products: 3.51 us -> none  [the longest x1 2.75 us: contract_last(): lax.dot_general(left, right, (((1,), (1,)), ((), ())), preferred_element_...]
    all_to_all x1 -> x0, starting transfers between devices: 3.39 us -> none  [on_device(): lax.all_to_all(picked.reshape(token_count, tp_count, depth), 'tp', split_...]
  transfers between devices with their start and end apart: 4 -> 0, of which waited for: 4 -> 0; matrix products, arithmetic and copies ran while one was open for 0% -> 0% of each run, Pallas kernels for 0% -> 0%
where the time goes in v1:
time: 69.8 us; the launch traced here: 69.3 us
  Pallas kernels  50.5 us (72%)
  local copies, waits for them, and re-layouts  8.76 us (13%)
  matrix products  5.49 us (8%)
  other arithmetic  4.26 us (6%)
    pallas_call x1, Pallas kernels, project(): pl.pallas_call(functools.partial(project_kernel, fsdp_count, tp_count), o...  28 us
    pallas_call x1, Pallas kernels, output(): pl.pallas_call(functools.partial(output_kernel, fsdp_count, tp_count), ou...  22.5 us
    gather x3, local copies, waits for them, and re-layouts, on_device(): picked = jnp.take(embedding, jnp.clip(shifted, 0, vocab_part - 1), axis=0)  5.84 us
    dot_general x1, matrix products, attend(): jnp.einsum('rsghd,rjgd->rsghj', grouped, old_keys, preferred_element_type...  3.98 us

profile of v1, /device:TPU:3, one launch (start us, length us, event | category | flops | bytes accessed | tf_op | source)
XLA Modules:
  0.0 69.3 jit_solution(15559330649232752116)
XLA Ops:
  0.0 0.8 %dynamic_slice.3 = f32[256]{0:T(256)S(1)} dynamic-slice(f32[8192]{0:T(1024)} %param.12, s32[]{:T(128)S(6)} %select_n.57), dynamic_slice_sizes={256} | dynamic-slice | bytes 2052 | tf_op jit(solution)/shard_map/dynamic_slice | solution.py:467
  0.8 0.7 compare_and_fusion.1
  1.5 0.7 subtract_clamp_fusion
  2.2 0.7 %add_convert_fusion.1 = f32[4,4]{1,0:T(4,128)S(1)} fusion(s32[4]{0:T(128)} %param.10), kind=kLoop, calls=%fused_computation.57 | loop fusion | flops 32 | bytes 80 | tf_op jit(solution)/shard_map/convert_element_type | solution.py:21
  2.9 0.1 convert_element_type.48
  3.0 0.1 copy.15
  3.1 0.1 reshape.350
  3.2 0.1 and.24
  3.3 0.1 copy.17
  3.4 0.1 min.20
  3.4 0.1 min.24
  3.5 0.1 min.22
  3.7 0.7 %iota_compare_fusion = pred[4,4096]{1,0:T(4,128)(4,1)S(1)} fusion(s32[4]{0:T(128)} %param.10), kind=kLoop, calls=%fused_computation.25 | loop fusion | flops 16384 | bytes 16400 | tf_op jit(solution)/shard_map/lt | solution.py:61
  4.4 0.1 multiply_cosine_fusion.1
  4.5 0.0 copy-start
  4.5 0.0 copy-start.2
  4.5 5.5 %gather_fusion = bf16[128,1024]{1,0:T(8,128)(2,1)S(1)} fusion(bf16[19008,1024]{1,0:T(8,128)(2,1)} %param.11, s32[1024]{0:T(1024)S(1)} %pad_clamp_fusion), kind=kCustom, calls=%fused_computation | custom fusion | bytes 524800 | tf_op jit(solution)/shard_map/jit(_take)/gather | solution.py:462
  10.0 0.2 multiply_reduce_fusion
  10.3 0.2 copy.20
  10.5 0.2 copy.21
  10.6 0.1 select_bitcast_fusion.picked
  10.8 0.0 copy-done
  10.8 0.0 copy-done.2
  10.8 28.0 %project.1 = f32[16,1280]{1,0:T(8,128)S(1)} custom-call(bf16[4,128,256]{2,1,0:T(8,128)(2,1)S(1)} %select_bitcast_fusion.picked, f32[8,128]{1,0:T(8,128)S(1)} %broadcast_in_dim.102.squares, f32[1,256]{1,0:T(1,128)S(1)} %bitcast.87, bf16[256,4096]{1,0:T(8,128)(2,1)S(1)} %copy-done, bf16[256,1024]{1,0:T(8,128)(2,1)S(1)} %copy-done.2), custom_call_target="tpu_custom_call" | custom-call | tf_op jit(solution)/shard_map/project/pallas_call | solution.py:271
  38.9 0.1 subtract_convert_fusion
  39.0 0.1 fusion.31
  39.1 0.3 select_reduce_fusion.1
  39.5 0.0 copy-start.3
  39.5 4.0 %select_reduce_fusion = (f32[4,4,8]{2,1,0:T(4,128)S(1)}, f32[4,1,4096,4,8]{2,4,3,0,1:T(8,128)S(1)}) fusion(pred[4,4096]{1,0:T(4,128)(4,1)S(1)} %iota_compare_fusion, bf16[4,4096,128]{2,1,0:T(8,128)(2,1)} %param.16, bf16[4,4,8,64]{3,2,1,0:T(8,128)(2,1)S(1)} %bitcast.93, bf16[4,4,8,64]{3,2,1,0:T(8,128)(2,1)S(1)} %bitcast.91), kind=kOutput, calls=%fused_computation.10 | convolution fusion | flops 135856000 | bytes 6341120 | tf_op jit(solution)/shard_map/rsghd,rjgd->rsghj/dot_general | solution.py:54
  43.5 0.1 fusion.20
  43.6 0.6 bitcast_reduce_fusion
  44.2 0.3 fusion.21
  44.4 0.0 copy-done.3
  44.4 0.0 copy-start.1
  44.4 0.9 %fusion.11 = bf16[4,128,4,8]{1,3,2,0:T(8,128)(2,1)S(1)} fusion(f32[4,128,4,8]{1,3,2,0:T(8,128)S(1)} %fusion.21, bf16[4,4096,128]{2,1,0:T(8,128)(2,1)S(1)} %copy-done.3, f32[4,1,4096,4,8]{2,4,3,0,1:T(8,128)S(1)} %get-tuple-element.12, f32[4,4,8]{2,1,0:T(4,128)S(1)} %add.75, f32[4,4,8]{2,1,0:T(4,128)S(1)} %max.12, pred[4,4096]{1,0:T(4,128)(4,1)S(1)} %iota_compare_fusion), kind=kOutput, calls=%fused_computation.13 | convolution fusion | flops 136347648 | bytes 6407168 | tf_op jit(solution)/shard_map/rsghj,rjgd->rsghd/dot_general | solution.py:75
  45.4 0.7 copy-done.1
  46.0 22.5 %output.1 = bf16[8,16,256]{2,1,0:T(8,128)(2,1)S(1)} custom-call(bf16[16,1024]{1,0:T(8,128)(2,1)S(1)} %bitcast.86, bf16[256,4096]{1,0:T(8,128)(2,1)S(1)} %copy-done.1), custom_call_target="tpu_custom_call" | custom-call | tf_op jit(solution)/shard_map/output/pallas_call | solution.py:423
  68.6 0.7 reshape.349
  (19 shorter events, 0.2 us)
Async XLA Ops:
  4.5 6.2 %copy-start = (bf16[256,4096]{1,0:T(8,128)(2,1)S(1)}, bf16[256,4096]{1,0:T(8,128)(2,1)}, u32[]{:S(2)}) copy-start(bf16[256,4096]{1,0:T(8,128)(2,1)} %w_query.1) | copy-start | bytes 6291460
  4.5 6.2 %copy-start.2 = (bf16[256,1024]{1,0:T(8,128)(2,1)S(1)}, bf16[256,1024]{1,0:T(8,128)(2,1)}, u32[]{:S(2)}) copy-start(bf16[256,1024]{1,0:T(8,128)(2,1)} %w_keyval.1) | copy-start | bytes 1572868
  39.5 5.0 %copy-start.3 = (bf16[4,4096,128]{2,1,0:T(8,128)(2,1)S(1)}, bf16[4,4096,128]{2,1,0:T(8,128)(2,1)}, u32[]{:S(2)}) copy-start(bf16[4,4096,128]{2,1,0:T(8,128)(2,1)} %param.17) | copy-start | bytes 12582916
  44.4 1.6 %copy-start.1 = (bf16[256,4096]{1,0:T(8,128)(2,1)S(1)}, bf16[256,4096]{1,0:T(8,128)(2,1)}, u32[]{:S(2)}) copy-start(bf16[256,4096]{1,0:T(8,128)(2,1)} %w_out.1) | copy-start | bytes 6291460

commit v2 on v1

v2 whole, which is shorter than its diff:
```python
import functools
import math

import jax
import jax.numpy as jnp
from jax import lax
from jax.experimental import pallas as pl
from jax.experimental.pallas import tpu as pltpu
from jax.sharding import PartitionSpec as P

HD = 128


EPS_NORM = 1e-06
ROPE_BASE = 1000000.0


def contract_last(left, right):
    return lax.dot_general(
        left, right, (((1,), (1,)), ((), ())), preferred_element_type=jnp.float32
    )


MESH = pl.DeviceIdType.MESH
VMEM_LIMIT = 48 * 1024 * 1024


def remote(src, dst, send_sem, recv_sem, device):
    return pltpu.make_async_remote_copy(
        src_ref=src,
        dst_ref=dst,
        send_sem=send_sem,
        recv_sem=recv_sem,
        device_id=device,
        device_id_type=MESH,
    )


def greet_all(me, count, tp_count):
    barrier = pltpu.get_barrier_semaphore()

    def greet(step, carry):
        other = lax.rem(me + step, count)
        pl.semaphore_signal(
            barrier, inc=1, device_id=(other // tp_count, lax.rem(other, tp_count)), device_id_type=MESH
        )
        return carry

    lax.fori_loop(1, count, greet, 0)
    pl.semaphore_wait(barrier, count - 1)


def attend_rows(
    projected, q_cols, kv_cols, lengths, cosine, sine_part, keys, values, key_copies, value_copies, attended
):
    tokens = projected.shape[0]
    row_dev, context, _ = keys.shape
    steps = tokens // row_dev
    heads = q_cols // HD
    lanes = heads * steps
    score_scale = 1.0 / math.sqrt(HD)

    def turned(lo):
        vectors = projected[:, lo : lo + HD]
        swapped = pltpu.roll(vectors, HD // 2, 1)
        return (vectors * cosine[...] + swapped * sine_part[...]).astype(jnp.bfloat16)

    queries = jnp.concatenate([turned(h * HD) for h in range(heads)], 0)
    new_keys = turned(q_cols)
    new_values = projected[:, q_cols + HD : q_cols + 2 * HD].astype(jnp.bfloat16)
    total_rows = heads * tokens
    pick_row = lax.broadcasted_iota(jnp.int32, (lanes, total_rows), 0)
    pick_col = lax.broadcasted_iota(jnp.int32, (lanes, total_rows), 1)
    picked_col = pick_row // steps * tokens + pick_row % steps
    new_row = lax.broadcasted_iota(jnp.int32, (lanes, tokens), 0) % steps
    new_col = lax.broadcasted_iota(jnp.int32, (lanes, tokens), 1)
    slots = lax.broadcasted_iota(jnp.int32, (lanes, context), 1)
    outs = []
    for r in range(row_dev):
        choose = jnp.where(pick_col == picked_col + r * steps, 1.0, 0.0).astype(jnp.bfloat16)
        query = jnp.dot(choose, queries, preferred_element_type=jnp.float32).astype(jnp.bfloat16)
        key_copies[r].wait()
        old_scores = contract_last(query, keys[r]) * score_scale
        new_scores = contract_last(query, new_keys) * score_scale
        step_of = new_col - r * steps
        old_scores = jnp.where(slots < lengths[r], old_scores, -jnp.inf)
        new_scores = jnp.where((step_of >= 0) & (step_of <= new_row), new_scores, -jnp.inf)
        largest = jnp.maximum(
            jnp.max(old_scores, -1, keepdims=True), jnp.max(new_scores, -1, keepdims=True)
        )
        old_weights = jnp.exp(old_scores - largest)
        new_weights = jnp.exp(new_scores - largest)
        share = 1.0 / (
            jnp.sum(old_weights, -1, keepdims=True) + jnp.sum(new_weights, -1, keepdims=True)
        )
        value_copies[r].wait()
        blended = jnp.dot(
            (old_weights * share).astype(jnp.bfloat16), values[r], preferred_element_type=jnp.float32
        ) + jnp.dot(
            (new_weights * share).astype(jnp.bfloat16), new_values, preferred_element_type=jnp.float32
        )
        outs.append(blended.astype(jnp.bfloat16))
    stacked = jnp.concatenate(outs, 0)
    back_row = lax.broadcasted_iota(jnp.int32, (total_rows, total_rows), 0)
    back_col = lax.broadcasted_iota(jnp.int32, (total_rows, total_rows), 1)
    token = back_row % tokens
    wanted = token // steps * lanes + back_row // tokens * steps + token % steps
    choose = jnp.where(back_col == wanted, 1.0, 0.0).astype(jnp.bfloat16)
    ordered = jnp.dot(choose, stacked, preferred_element_type=jnp.float32).astype(jnp.bfloat16)
    for h in range(heads):
        attended[:, h * HD : (h + 1) * HD] = ordered[h * tokens : (h + 1) * tokens]


def block_kernel(
    fsdp_count, tp_count, lengths, picked, squares, gain, cosine, sine_part, w_query, w_keyval, w_out, key_cache,
    value_cache, got,
    wq_buf, wkv_buf, x_buf, sq_buf, away, kept, from_core, plane_out, from_plane, line_out, from_line,
    w_buf, parts, sums, blocks, gathered, keys, values,
    w_sem, cache_sem, x_send, x_recv, sq_send, sq_recv, core_send, core_recv, plane_send, plane_recv,
    line_send, line_recv, aline_send, aline_recv, aplane_send, aplane_recv, acore_send, acore_recv,
    out_send, out_recv,
):
    f = lax.axis_index("fsdp")
    t = lax.axis_index("tp")
    count = fsdp_count * tp_count
    me = f * tp_count + t
    fz, fy = f // 2, lax.rem(f, 2)
    xi, core = t // 2, lax.rem(t, 2)
    lines = fsdp_count // 2
    query_copy = pltpu.make_async_copy(w_query, wq_buf, w_sem.at[0])
    keyval_copy = pltpu.make_async_copy(w_keyval, wkv_buf, w_sem.at[1])
    query_copy.start()
    keyval_copy.start()
    key_copies = [
        pltpu.make_async_copy(key_cache.at[r], keys.at[r], cache_sem.at[0, r])
        for r in range(keys.shape[0])
    ]
    value_copies = [
        pltpu.make_async_copy(value_cache.at[r], values.at[r], cache_sem.at[1, r])
        for r in range(keys.shape[0])
    ]
    weight_copy = pltpu.make_async_copy(w_out, w_buf, w_sem.at[2])
    for copy in key_copies + value_copies + [weight_copy]:
        copy.start()
    greet_all(me, count, tp_count)

    def x_copy(step):
        other = lax.rem(t + step, tp_count)
        return remote(
            picked.at[other], x_buf.at[step - 1], x_send.at[step - 1], x_recv.at[step - 1], (f, other)
        )

    def sq_copy(step):
        other = lax.rem(me + step, count)
        return remote(
            squares, sq_buf.at[step - 1], sq_send.at[step - 1], sq_recv.at[step - 1],
            (other // tp_count, lax.rem(other, tp_count)),
        )

    for step in range(1, tp_count):
        x_copy(step).start()

    def send_sq(step, carry):
        sq_copy(step).start()
        return carry

    lax.fori_loop(1, count, send_sq, 0)
    inputs = picked[t].astype(jnp.float32)
    for step in range(1, tp_count):
        x_copy(step).wait_recv()
        inputs = inputs + x_buf[step - 1].astype(jnp.float32)

    def take_sq(step, total):
        sq_copy(step).wait_recv()
        return total + sq_buf[step - 1]

    total = lax.fori_loop(1, count, take_sq, squares[...])
    tokens, depth = inputs.shape
    column = jnp.transpose(jnp.broadcast_to(total[:1], (128, tokens)))[:, :1]
    scale_rows = lax.rsqrt(column / (depth * count) + EPS_NORM)
    normed = (inputs * scale_rows * gain[...]).astype(jnp.bfloat16)
    query_copy.wait()
    keyval_copy.wait()
    q_cols = wq_buf.shape[1] // tp_count
    kv_cols = wkv_buf.shape[1] // tp_count

    def project(head, store):
        for lo in range(0, q_cols, 512):
            columns = pl.ds(pl.multiple_of(head * q_cols + lo, 128), min(512, q_cols - lo))
            store(lo, jnp.dot(normed, wq_buf[:, columns], preferred_element_type=jnp.float32))
        columns = pl.ds(pl.multiple_of(head * kv_cols, 128), kv_cols)
        store(q_cols, jnp.dot(normed, wkv_buf[:, columns], preferred_element_type=jnp.float32))

    def core_copy(side):
        return remote(
            away.at[side], from_core.at[side], core_send.at[side], core_recv.at[side], (f, xi * 2 + 1 - core)
        )

    order = (lax.rem(xi + 1, 2), xi)
    for place in range(2):
        def store(lo, value, place=place):
            away[place, :, lo : lo + value.shape[1]] = value.astype(jnp.bfloat16)

        project(order[place] * 2 + 1 - core, store)
        core_copy(place).start()

    for place in range(2):
        def store(lo, value, place=place):
            kept[place, :, lo : lo + value.shape[1]] = value

        project(order[place] * 2 + core, store)
    half = tokens // 2

    def plane_copy(dx, dy):
        slot = dx * 2 + dy - 1
        return remote(
            plane_out.at[slot], from_plane.at[slot], plane_send.at[slot], plane_recv.at[slot],
            (fz * 2 + lax.rem(fy + dy, 2), lax.rem(xi + dx, 2) * 2 + core),
        )

    core_copy(0).wait_recv()
    for dy in (1, 0):
        rows = pl.ds(pl.multiple_of(lax.rem(fy + dy, 2) * half, 16), half)
        plane_out[2 + dy - 1] = (
            kept[0, rows, :] + from_core[0, rows, :].astype(jnp.float32)
        ).astype(jnp.bfloat16)
        plane_copy(1, dy).start()
    core_copy(1).wait_recv()
    rows = pl.ds(pl.multiple_of(lax.rem(fy + 1, 2) * half, 16), half)
    plane_out[0] = (kept[1, rows, :] + from_core[1, rows, :].astype(jnp.float32)).astype(jnp.bfloat16)
    plane_copy(0, 1).start()
    rows = pl.ds(pl.multiple_of(fy * half, 16), half)
    own = kept[1, rows, :] + from_core[1, rows, :].astype(jnp.float32)
    plane_copy(0, 1).wait_recv()
    own = own + from_plane[0].astype(jnp.float32)
    plane_copy(1, 0).wait_recv()
    own = own + from_plane[1].astype(jnp.float32)
    plane_copy(1, 1).wait_recv()
    own = own + from_plane[2].astype(jnp.float32)
    block = half // lines
    kept[0, :half, :] = own
    line_out[...] = own.astype(jnp.bfloat16).reshape(line_out.shape)

    def line_copy(step):
        other = lax.rem(fz + step, lines)
        return remote(
            line_out.at[other], from_line.at[step - 1], line_send.at[step - 1], line_recv.at[step - 1],
            (other * 2 + fy, t),
        )

    for step in range(1, lines):
        line_copy(step).start()
    result = kept[0, pl.ds(pl.multiple_of(fz * block, 16), block), :]
    for step in range(1, lines):
        line_copy(step).wait_recv()
        result = result + from_line[step - 1].astype(jnp.float32)
    attend_rows(
        result, q_cols, kv_cols, lengths, cosine, sine_part, keys, values, key_copies, value_copies,
        parts.at[core, xi, fy, fz],
    )
    near = fsdp_count // tp_count
    def aline_copy(step, source):
        other = lax.rem(fz + step, lines)
        spot = parts.at[core, xi, fy, source]
        return remote(spot, spot, aline_send.at[step - 1], aline_recv.at[step - 1], (other * 2 + fy, t))

    def aplane_copy(dx, dy, back):
        slot = dx * 2 + dy - 1
        other_x, other_y = lax.rem(xi + dx, 2), lax.rem(fy + dy, 2)
        spot = parts.at[core, other_x, other_y] if back else parts.at[core, xi, fy]
        return remote(
            spot, spot, aplane_send.at[slot], aplane_recv.at[slot], (fz * 2 + other_y, other_x * 2 + core)
        )

    def acore_copy(dx, dy, back):
        slot = dx * 2 + dy
        side = 1 - core if back else core
        spot = parts.at[side, lax.rem(xi + dx, 2), lax.rem(fy + dy, 2)]
        return remote(spot, spot, acore_send.at[slot], acore_recv.at[slot], (f, xi * 2 + 1 - core))

    for step in range(1, lines):
        aline_copy(step, fz).start()
    for step in range(1, lines):
        aline_copy(step, lax.rem(fz - step + lines, lines)).wait_recv()
    peers = ((1, 1), (1, 0), (0, 1))
    for dx, dy in peers:
        aplane_copy(dx, dy, False).start()
    acore_copy(0, 0, False).start()
    for dx, dy in reversed(peers):
        aplane_copy(dx, dy, True).wait_recv()
        acore_copy(dx, dy, False).start()
    weight_copy.wait()
    cols = w_buf.shape[1] // tp_count

    def add(side, far, first):
        columns = pl.ds(pl.multiple_of((far * 2 + side) * cols, 128), cols)
        value = contract_last(parts[side, far].reshape(tokens, cols), w_buf[:, columns])
        if first:
            sums[...] = value
        else:
            sums[...] += value

    add(core, xi, True)
    add(core, lax.rem(xi + 1, 2), False)
    for dx, dy in ((0, 0),) + tuple(reversed(peers)):
        acore_copy(dx, dy, True).wait_recv()
    add(1 - core, xi, False)
    add(1 - core, lax.rem(xi + 1, 2), False)
    blocks[...] = sums[...].astype(jnp.bfloat16).reshape(blocks.shape)
    target = f // near
    place = lax.rem(f, near) * tp_count + t

    def out_copy(step):
        other = lax.rem(f + step, fsdp_count)
        return remote(
            blocks.at[lax.rem(other, 2) * lines + other // 2], gathered.at[place],
            out_send.at[step], out_recv.at[place], (other, target),
        )

    for step in range(1, fsdp_count):
        out_copy(step).start()

    @pl.when(target != t)
    def _():
        out_copy(0).start()

    @pl.when(target == t)
    def _():
        gathered[place] = blocks[fy * lines + fz]

    def source(slot):
        return t * near + slot // tp_count, slot % tp_count

    for slot in range(near * tp_count):
        sender_f, sender_t = source(slot)

        @pl.when(jnp.logical_or(sender_f != f, sender_t != t))
        def _(slot=slot, sender_f=sender_f, sender_t=sender_t):
            remote(
                blocks.at[0], gathered.at[slot], out_send.at[0], out_recv.at[slot], (sender_f, sender_t)
            ).wait_recv()

    got[...] = gathered[...]
    for step in range(1, lines):
        aline_copy(step, fz).wait_send()
    for dx, dy in peers:
        aplane_copy(dx, dy, False).wait_send()
    for dx, dy in ((0, 0),) + peers:
        acore_copy(dx, dy, False).wait_send()
    for step in range(1, fsdp_count):
        out_copy(step).wait_send()

    @pl.when(target != t)
    def _():
        out_copy(0).wait_send()
    for step in range(1, tp_count):
        x_copy(step).wait_send()

    def done_sq(step, carry):
        sq_copy(step).wait_send()
        return carry

    lax.fori_loop(1, count, done_sq, 0)
    for place in range(2):
        core_copy(place).wait_send()
    plane_copy(0, 1).wait_send()
    plane_copy(1, 0).wait_send()
    plane_copy(1, 1).wait_send()
    for step in range(1, lines):
        line_copy(step).wait_send()


def block(
    fsdp_count, tp_count, lengths, picked, squares, gain, cosine, sine_part, w_query, w_keyval, w_out,
    key_cache, value_cache
):
    _, tokens, depth = picked.shape
    count = fsdp_count * tp_count
    lines = fsdp_count // 2
    cols = (w_query.shape[1] + w_keyval.shape[1]) // tp_count
    half = tokens // 2
    row_tokens = tokens // fsdp_count
    out_cols = w_out.shape[1] // tp_count
    slots = fsdp_count // tp_count * tp_count
    dma = pltpu.SemaphoreType.DMA
    bf16, f32 = jnp.bfloat16, jnp.float32
    vmem = pl.BlockSpec(memory_space=pltpu.VMEM)
    hbm = pl.BlockSpec(memory_space=pltpu.HBM)
    return pl.pallas_call(
        functools.partial(block_kernel, fsdp_count, tp_count),
        out_shape=jax.ShapeDtypeStruct((slots, row_tokens, depth), bf16),
        in_specs=[pl.BlockSpec(memory_space=pltpu.SMEM)] + [vmem] * 5 + [hbm] * 5,
        out_specs=vmem,
        scratch_shapes=[
            pltpu.VMEM(w_query.shape, bf16),
            pltpu.VMEM(w_keyval.shape, bf16),
            pltpu.VMEM((tp_count - 1, tokens, depth), bf16),
            pltpu.VMEM((count - 1,) + squares.shape, f32),
            pltpu.VMEM((2, tokens, cols), bf16),
            pltpu.VMEM((2, tokens, cols), f32),
            pltpu.VMEM((2, tokens, cols), bf16),
            pltpu.VMEM((3, half, cols), bf16),
            pltpu.VMEM((3, half, cols), bf16),
            pltpu.VMEM((lines, half // lines, cols), bf16),
            pltpu.VMEM((lines - 1, half // lines, cols), bf16),
            pltpu.VMEM(w_out.shape, bf16),
            pltpu.VMEM((2, 2, 2, lines, row_tokens, out_cols), bf16),
            pltpu.VMEM((tokens, depth), f32),
            pltpu.VMEM((fsdp_count, row_tokens, depth), bf16),
            pltpu.VMEM((slots, row_tokens, depth), bf16),
            pltpu.VMEM(key_cache.shape, bf16),
            pltpu.VMEM(value_cache.shape, bf16),
            dma((3,)), dma((2, key_cache.shape[0])),
            dma((tp_count - 1,)), dma((tp_count - 1,)),
            dma((count - 1,)), dma((count - 1,)),
            dma((2,)), dma((2,)),
            dma((3,)), dma((3,)),
            dma((lines - 1,)), dma((lines - 1,)),
            dma((lines - 1,)), dma((lines - 1,)),
            dma((3,)), dma((3,)),
            dma((4,)), dma((4,)),
            dma((fsdp_count,)), dma((slots,)),
        ],
        compiler_params=pltpu.CompilerParams(
            collective_id=0, has_side_effects=True, vmem_limit_bytes=VMEM_LIMIT
        ),
        name="block",
    )(
        lengths, picked, squares, gain, cosine, sine_part, w_query, w_keyval, w_out, key_cache, value_cache
    )


def on_device(
    token_ids, lengths, embedding, norm_gain, w_query, w_keyval, w_out, key_cache, value_cache
):
    tp_count = lax.axis_size("tp")
    fsdp_count = lax.axis_size("fsdp")
    tp_rank = lax.axis_index("tp")
    fsdp_rank = lax.axis_index("fsdp")
    step_count = token_ids.shape[1]
    row_dev = lengths.shape[0]
    vocab_part = embedding.shape[0]
    token_count = token_ids.size
    depth = w_query.shape[0]
    ordered = token_ids.reshape(fsdp_count // 2, 2, -1).transpose(1, 0, 2).reshape(-1)
    shifted = ordered - tp_rank * vocab_part
    picked = embedding.at[shifted].get(mode="fill", fill_value=0, wrap_negative_indices=False)
    wide = picked.astype(jnp.float32)
    squares = jnp.broadcast_to(jnp.sum(wide * wide, -1)[None, :], (8, token_count))
    picked = picked.reshape(token_count, tp_count, depth).transpose(1, 0, 2)
    gain = lax.dynamic_slice(norm_gain, ((fsdp_rank * tp_count + tp_rank) * depth,), (depth,))
    positions = (lengths[:, None] + jnp.arange(step_count, dtype=jnp.int32)[None, :]).reshape(-1)
    midpoint = HD // 2
    frequency = ROPE_BASE ** (-2.0 * jnp.arange(midpoint, dtype=jnp.float32) / HD)
    angles = positions.astype(jnp.float32)[:, None] * frequency
    cosine = jnp.cos(angles)
    sine_part = jnp.sin(angles)
    rows = block(
        fsdp_count, tp_count, lengths, picked, squares, gain[None, :],
        jnp.concatenate([cosine, cosine], -1), jnp.concatenate([-sine_part, sine_part], -1),
        w_query, w_keyval, w_out, key_cache, value_cache,
    )
    return rows.transpose(1, 0, 2).reshape(row_dev, step_count, -1)


def solution(mesh):
    return jax.shard_map(
        on_device,
        mesh=mesh,
        in_specs=(
            P(),
            P("fsdp"),
            P("tp", "fsdp"),
            P(),
            P(("fsdp", "tp"), None),
            P(("fsdp", "tp"), None),
            P(("fsdp", "tp"), None),
            P("fsdp", None, "tp"),
            P("fsdp", None, "tp"),
        ),
        out_specs=P("fsdp", None, "tp"),
        check_vma=False,
    )
```

time: 69.8 us -> 64.2 us (0.920)
  matrix products: 5.49 us -> 0 us
  other arithmetic: 4.26 us -> 1.94 us
  Pallas kernels: 50.5 us -> 52.4 us
    dot_general x4 -> x0, matrix products: 5.49 us -> none  [the longest x1 3.98 us: attend(): jnp.einsum('rsghd,rjgd->rsghj', grouped, old_keys, preferred_element_type...]
    pallas_call x2 -> x1, Pallas kernels: 50.5 us -> 52.4 us  [block(): pl.pallas_call(functools.partial(block_kernel, fsdp_count, tp_count), out...]
    unnamed x12 -> x8, local copies, waits for them, and re-layouts: 0.71 us -> 1.6 us
    lt x1 -> x0, other arithmetic: 0.75 us -> none  [attend(): jnp.arange(context, dtype=jnp.int32)[None, :] < lengths[:, None]]
where the time goes in v2:
time: 64.2 us; the launch traced here: 63.9 us
  Pallas kernels  52.4 us (82%)
  local copies, waits for them, and re-layouts  9.35 us (15%)
  other arithmetic  1.94 us (3%)
    pallas_call x1, Pallas kernels, block(): pl.pallas_call(functools.partial(block_kernel, fsdp_count, tp_count), out...  52.4 us
    gather x3, local copies, waits for them, and re-layouts, on_device(): embedding.at[shifted]  5.51 us
    unnamed x8, local copies, waits for them, and re-layouts  1.6 us

profile of v2, /device:TPU:3, one launch (start us, length us, event | category | flops | bytes accessed | tf_op | source)
XLA Modules:
  0.0 63.9 jit_solution(5543993118444246626)
XLA Ops:
  0.0 0.0 copy-start.3
  0.0 0.0 copy-start.2
  0.0 0.0 copy-start
  0.0 0.9 %dynamic_slice.3 = f32[256]{0:T(256)S(1)} dynamic-slice(f32[8192]{0:T(1024)} %param.12, s32[]{:T(128)S(6)} %select_n.11), dynamic_slice_sizes={256} | dynamic-slice | bytes 2052 | tf_op jit(solution)/shard_map/dynamic_slice | solution.py:451
  0.9 0.7 %add_convert_fusion = f32[4,4]{1,0:T(4,128)S(1)} fusion(s32[4]{0:T(128)} %lengths.1), kind=kLoop, calls=%fused_computation.9 | loop fusion | flops 32 | bytes 80 | tf_op jit(solution)/shard_map/convert_element_type | solution.py:455
  1.7 0.1 convert_element_type.15
  1.8 0.7 %compare_and_fusion = (pred[32,4]{0,1:T(4,128)(4,1)S(1)}, s32[32,4]{0,1:T(4,128)S(1)}) fusion(s32[32,4]{0,1:T(4,128)} %param.9, s32[]{:T(128)S(6)} %mul.28), kind=kLoop, calls=%fused_computation.10 | loop fusion | flops 512 | bytes 1156 | tf_op jit(solution)/shard_map/and | solution.py:447
  2.4 0.1 copy.14
  2.6 0.1 reshape.67
  2.7 0.1 and.16
  2.7 0.1 copy.16
  2.8 0.1 sub.29
  2.9 0.1 reshape.70
  3.0 0.1 fusion
  3.1 0.1 pad_maximum_fusion
  3.2 5.2 %gather_fusion = bf16[128,1024]{1,0:T(8,128)(2,1)S(1)} fusion(bf16[19008,1024]{1,0:T(8,128)(2,1)} %param.11, s32[1024]{0:T(1024)S(1)} %pad_clamp_fusion), kind=kCustom, calls=%fused_computation | custom fusion | bytes 524800 | tf_op jit(solution)/shard_map/gather | solution.py:447
  8.4 0.2 multiply_reduce_fusion
  8.6 0.2 copy.18
  8.8 0.2 copy.19
  9.0 0.1 select_bitcast_fusion.picked
  9.1 0.0 copy-done.3
  9.1 0.0 copy-done.2
  9.1 0.0 copy-done
  9.1 0.0 copy-start.1
  9.1 1.6 %copy-done.1 = bf16[256,4096]{1,0:T(8,128)(2,1)S(1)} copy-done((bf16[256,4096]{1,0:T(8,128)(2,1)S(1)}, bf16[256,4096]{1,0:T(8,128)(2,1)}, u32[]{:S(2)}) %copy-start.1) | copy-done | bytes 2097176
  10.7 52.4 %block.1 = bf16[8,16,256]{2,1,0:T(8,128)(2,1)S(1)} custom-call(s32[4]{0:T(128)S(1)} %copy-done.3, bf16[4,128,256]{2,1,0:T(8,128)(2,1)S(1)} %select_bitcast_fusion.picked, f32[8,128]{1,0:T(8,128)S(1)} %broadcast_in_dim.28.squares, f32[1,256]{1,0:T(1,128)S(1)} %bitcast.8, f32[16,128]{1,0:T(8,128)S(1)} %get-tuple-element.10.cosine, ...), custom_call_target="tpu_custom_call" | custom-call | tf_op jit(solution)/shard_map/block/pallas_call | solution.py:389
  63.2 0.7 %reshape.66 = bf16[4,4,2048]{2,1,0:T(4,128)(2,1)} reshape(bf16[16,8,256]{2,1,0:T(8,128)(2,1)S(1)} %copy.20) | data formatting | bytes 131072 | tf_op jit(solution)/shard_map/reshape | solution.py:463
  (6 shorter events, 0.1 us)
Async XLA Ops:
  0.0 9.1 %copy-start.3 = (s32[4]{0:T(128)S(1)}, s32[4]{0:T(128)}, u32[]{:S(2)}) copy-start(s32[4]{0:T(128)} %lengths.1) | copy-start | bytes 52
  0.0 9.1 %copy-start.2 = (bf16[256,1024]{1,0:T(8,128)(2,1)S(1)}, bf16[256,1024]{1,0:T(8,128)(2,1)}, u32[]{:S(2)}) copy-start(bf16[256,1024]{1,0:T(8,128)(2,1)} %w_keyval.1) | copy-start | bytes 1572868
  0.0 9.1 %copy-start = (bf16[256,4096]{1,0:T(8,128)(2,1)S(1)}, bf16[256,4096]{1,0:T(8,128)(2,1)}, u32[]{:S(2)}) copy-start(bf16[256,4096]{1,0:T(8,128)(2,1)} %w_query.1) | copy-start | bytes 6291460
  9.1 1.6 %copy-start.1 = (bf16[256,4096]{1,0:T(8,128)(2,1)S(1)}, bf16[256,4096]{1,0:T(8,128)(2,1)}, u32[]{:S(2)}) copy-start(bf16[256,4096]{1,0:T(8,128)(2,1)} %w_out.1) | copy-start | bytes 6291460

commit v3 on v2

--- a/solution.py
+++ b/solution.py
@@ -264,12 +264,14 @@
         spot = parts.at[core, xi, fy, source]
         return remote(spot, spot, aline_send.at[step - 1], aline_recv.at[step - 1], (other * 2 + fy, t))
 
-    def aplane_copy(dx, dy, back):
+    def aplane_copy(dx, dy, step, back):
         slot = dx * 2 + dy - 1
         other_x, other_y = lax.rem(xi + dx, 2), lax.rem(fy + dy, 2)
-        spot = parts.at[core, other_x, other_y] if back else parts.at[core, xi, fy]
-        return remote(
-            spot, spot, aplane_send.at[slot], aplane_recv.at[slot], (fz * 2 + other_y, other_x * 2 + core)
+        piece = lax.rem(fz - step + lines, lines)
+        spot = parts.at[core, other_x, other_y, piece] if back else parts.at[core, xi, fy, piece]
+        return remote(
+            spot, spot, aplane_send.at[slot, step], aplane_recv.at[slot, step],
+            (fz * 2 + other_y, other_x * 2 + core),
         )
 
     def acore_copy(dx, dy, back):
@@ -280,14 +282,16 @@
 
     for step in range(1, lines):
         aline_copy(step, fz).start()
-    for step in range(1, lines):
-        aline_copy(step, lax.rem(fz - step + lines, lines)).wait_recv()
     peers = ((1, 1), (1, 0), (0, 1))
-    for dx, dy in peers:
-        aplane_copy(dx, dy, False).start()
+    for step in range(lines):
+        if step > 0:
+            aline_copy(step, lax.rem(fz - step + lines, lines)).wait_recv()
+        for dx, dy in peers:
+            aplane_copy(dx, dy, step, False).start()
     acore_copy(0, 0, False).start()
     for dx, dy in reversed(peers):
-        aplane_copy(dx, dy, True).wait_recv()
+        for step in range(lines):
+            aplane_copy(dx, dy, step, True).wait_recv()
         acore_copy(dx, dy, False).start()
     weight_copy.wait()
     cols = w_buf.shape[1] // tp_count
@@ -344,7 +348,8 @@
     for step in range(1, lines):
         aline_copy(step, fz).wait_send()
     for dx, dy in peers:
-        aplane_copy(dx, dy, False).wait_send()
+        for step in range(lines):
+            aplane_copy(dx, dy, step, False).wait_send()
     for dx, dy in ((0, 0),) + peers:
         acore_copy(dx, dy, False).wait_send()
     for step in range(1, fsdp_count):
@@ -417,7 +422,7 @@
             dma((3,)), dma((3,)),
             dma((lines - 1,)), dma((lines - 1,)),
             dma((lines - 1,)), dma((lines - 1,)),
-            dma((3,)), dma((3,)),
+            dma((3, lines)), dma((3, lines)),
             dma((4,)), dma((4,)),
             dma((fsdp_count,)), dma((slots,)),
         ],

time: 64.2 us -> 61.9 us (0.964)
  Pallas kernels: 52.4 us -> 49.5 us
    pallas_call x1, Pallas kernels: 52.4 us -> 49.5 us  [block(): pl.pallas_call(functools.partial(block_kernel, fsdp_count, tp_count), out...]
where the time goes in v3:
time: 61.9 us; the launch traced here: 61.1 us
  Pallas kernels  49.5 us (80%)
  local copies, waits for them, and re-layouts  9.58 us (15%)
  other arithmetic  1.94 us (3%)
    pallas_call x1, Pallas kernels, block(): pl.pallas_call(functools.partial(block_kernel, fsdp_count, tp_count), out...  49.5 us
    gather x3, local copies, waits for them, and re-layouts, on_device(): embedding.at[shifted]  5.74 us
    unnamed x8, local copies, waits for them, and re-layouts  1.6 us

profile of v3, /device:TPU:3, one launch (start us, length us, event | category | flops | bytes accessed | tf_op | source)
XLA Modules:
  0.0 61.1 jit_solution(15893236251691710101)
XLA Ops:
  0.0 0.0 copy-start.3
  0.0 0.0 copy-start.2
  0.0 0.0 copy-start
  0.0 0.9 %dynamic_slice.3 = f32[256]{0:T(256)S(1)} dynamic-slice(f32[8192]{0:T(1024)} %param.12, s32[]{:T(128)S(6)} %select_n.11), dynamic_slice_sizes={256} | dynamic-slice | bytes 2052 | tf_op jit(solution)/shard_map/dynamic_slice | solution.py:456
  0.9 0.7 %add_convert_fusion = f32[4,4]{1,0:T(4,128)S(1)} fusion(s32[4]{0:T(128)} %lengths.1), kind=kLoop, calls=%fused_computation.9 | loop fusion | flops 32 | bytes 80 | tf_op jit(solution)/shard_map/convert_element_type | solution.py:460
  1.7 0.1 convert_element_type.15
  1.8 0.7 %compare_and_fusion = (pred[32,4]{0,1:T(4,128)(4,1)S(1)}, s32[32,4]{0,1:T(4,128)S(1)}) fusion(s32[32,4]{0,1:T(4,128)} %param.9, s32[]{:T(128)S(6)} %mul.28), kind=kLoop, calls=%fused_computation.10 | loop fusion | flops 512 | bytes 1156 | tf_op jit(solution)/shard_map/and | solution.py:452
  2.4 0.1 copy.14
  2.6 0.1 reshape.67
  2.7 0.1 and.16
  2.7 0.1 copy.16
  2.8 0.1 sub.29
  2.9 0.1 reshape.70
  3.0 0.1 fusion
  3.1 0.1 pad_maximum_fusion
  3.2 5.4 %gather_fusion = bf16[128,1024]{1,0:T(8,128)(2,1)S(1)} fusion(bf16[19008,1024]{1,0:T(8,128)(2,1)} %param.11, s32[1024]{0:T(1024)S(1)} %pad_clamp_fusion), kind=kCustom, calls=%fused_computation | custom fusion | bytes 524800 | tf_op jit(solution)/shard_map/gather | solution.py:452
  8.6 0.2 multiply_reduce_fusion
  8.8 0.2 copy.18
  9.0 0.2 copy.19
  9.2 0.1 select_bitcast_fusion.picked
  9.3 0.0 copy-done.3
  9.3 0.0 copy-done.2
  9.3 0.0 copy-done
  9.3 0.0 copy-start.1
  9.3 1.6 %copy-done.1 = bf16[256,4096]{1,0:T(8,128)(2,1)S(1)} copy-done((bf16[256,4096]{1,0:T(8,128)(2,1)S(1)}, bf16[256,4096]{1,0:T(8,128)(2,1)}, u32[]{:S(2)}) %copy-start.1) | copy-done | bytes 2097176
  10.9 49.5 %block.1 = bf16[8,16,256]{2,1,0:T(8,128)(2,1)S(1)} custom-call(s32[4]{0:T(128)S(1)} %copy-done.3, bf16[4,128,256]{2,1,0:T(8,128)(2,1)S(1)} %select_bitcast_fusion.picked, f32[8,128]{1,0:T(8,128)S(1)} %broadcast_in_dim.28.squares, f32[1,256]{1,0:T(1,128)S(1)} %bitcast.8, f32[16,128]{1,0:T(8,128)S(1)} %get-tuple-element.10.cosine, ...), custom_call_target="tpu_custom_call" | custom-call | tf_op jit(solution)/shard_map/block/pallas_call | solution.py:394
  60.5 0.7 %reshape.66 = bf16[4,4,2048]{2,1,0:T(4,128)(2,1)} reshape(bf16[16,8,256]{2,1,0:T(8,128)(2,1)S(1)} %copy.20) | data formatting | bytes 131072 | tf_op jit(solution)/shard_map/reshape | solution.py:468
  (6 shorter events, 0.1 us)
Async XLA Ops:
  0.0 9.3 %copy-start.3 = (s32[4]{0:T(128)S(1)}, s32[4]{0:T(128)}, u32[]{:S(2)}) copy-start(s32[4]{0:T(128)} %lengths.1) | copy-start | bytes 52
  0.0 9.3 %copy-start.2 = (bf16[256,1024]{1,0:T(8,128)(2,1)S(1)}, bf16[256,1024]{1,0:T(8,128)(2,1)}, u32[]{:S(2)}) copy-start(bf16[256,1024]{1,0:T(8,128)(2,1)} %w_keyval.1) | copy-start | bytes 1572868
  0.0 9.3 %copy-start = (bf16[256,4096]{1,0:T(8,128)(2,1)S(1)}, bf16[256,4096]{1,0:T(8,128)(2,1)}, u32[]{:S(2)}) copy-start(bf16[256,4096]{1,0:T(8,128)(2,1)} %w_query.1) | copy-start | bytes 6291460
  9.3 1.6 %copy-start.1 = (bf16[256,4096]{1,0:T(8,128)(2,1)S(1)}, bf16[256,4096]{1,0:T(8,128)(2,1)}, u32[]{:S(2)}) copy-start(bf16[256,4096]{1,0:T(8,128)(2,1)} %w_out.1) | copy-start | bytes 6291460
